TPU v7x, 512 devices: a whole 4x4x16 slice. The times are simulated.
512 devices in a mesh: inst: 64 (over z, x), tp: 8 (over y, core).
Axes of the slice: x: 4, y: 4, z: 16, core: 2. Of those that a mesh axis runs over, the one named last changes fastest.
Arguments:
- cached_state: bfloat16 [128, 8192, 128], P('inst', 'tp'), may hold values from -5 to 5
- kv_pool: bfloat16 [4096, 16, 2048], P('inst', None, 'tp'), may hold values from -5 to 5
- page_table: int32 [128, 32], P('inst'), may hold values from 0 to 63, as said below
- cached_len: int32 [128], replicated, may hold values from 1 to 512
- source_session: int32 [64], replicated, may hold values from 0 to 127, as said below
- turn_len: int32 [64], P('inst'), may hold values from 32 to 128
- x_inner: bfloat16 [8192, 8192], P('inst', 'tp'), may hold values from -80 to 80
- gate_z: bfloat16 [8192, 8192], P('inst', 'tp'), may hold values from -4 to 4
- b_proj: bfloat16 [8192, 1024], P('inst', 'tp'), may hold values from -0.29882812 to 0.29882812
- c_proj: bfloat16 [8192, 1024], P('inst', 'tp'), may hold values from -3 to 3
- step_size: float32 [128, 8192], P('tp', 'inst'), may hold values from 0 to 80, as said below
- decay_rate: float32 [128], P('tp'), may hold values from 0 to 1, as said below
- skip_gain: float32 [128], P('tp'), may hold values from 0.5 to 1.5
- norm_gain: float32 [8192], P('tp'), may hold values from 0.5 to 1.5
- queries: bfloat16 [8192, 8192], P('inst', 'tp'), may hold values from -16 to 16
- new_kv: bfloat16 [8192, 2048], P('inst', 'tp'), may hold values from -5 to 5
Outputs:
- mixer_out: bfloat16 [8192, 8192], P('inst', 'tp')
- attn_out: bfloat16 [8192, 8192], P('inst', 'tp')
- new_state: bfloat16 [64, 8192, 128], P('inst', 'tp')
Inputs may be any that keep to these rules, and one draw needn't show every extreme that they name: `page_table`: each instance's 2 x 32 entries are a permutation of its 64 page indices. `source_session`: stored session ids; every instance serves one session, and exactly one of each instance's 2 stored sessions is served. `step_size`: positive. `decay_rate`: positive.
All inputs are finite; a program needn't handle non-finite values.
Results may differ from a plain program's by a relative error of at most 0.0049.
Values may be sent and summed in bfloat16 or wider, within the bound.
A program may use at most 64 MiB of HBM per device.

v0:
```python
import jax
import jax.numpy as jnp
from jax import lax
from jax.sharding import PartitionSpec as P

HEAD_DIM = 64
KV_DIM = 128
SPAN = 128


exact_mode = lax.Precision.HIGHEST
EPSILON = 1e-05


def mixer_rows(
    x_inner,
    gate_z,
    b_proj,
    c_proj,
    step_size,
    decay_rate,
    skip_gain,
    norm_gain,
    start_state,
    length,
):
    turn_rows = x_inner.shape[0]
    inner_width = x_inner.shape[1]
    head_count = step_size.shape[0]
    state_dim = b_proj.shape[1]
    positions = jnp.arange(turn_rows, dtype=jnp.int32)
    live_rows = positions < length
    dt_live = jnp.where(live_rows[None, :], step_size, jnp.float32(0.0))
    log_decay = -dt_live * decay_rate[:, None]
    x_heads = x_inner.reshape(turn_rows, head_count, HEAD_DIM)
    lower_mask = positions[:SPAN, None] >= positions[None, :SPAN]
    lower_ones = lower_mask.astype(jnp.float32)
    state_now = start_state
    cumulative = jnp.dot(log_decay, lower_ones.T, precision=exact_mode)
    differ = cumulative[:, :, None] - cumulative[:, None, :]
    decay_table = jnp.where(
        lower_mask[None], jnp.exp(jnp.where(lower_mask[None], differ, 0.0)), 0.0
    )
    products = jnp.dot(c_proj, b_proj.T, preferred_element_type=jnp.float32)
    weights = (products[None] * decay_table * dt_live[:, None, :]).astype(jnp.bfloat16)
    intra = jnp.einsum("hij,jhp->ihp", weights, x_heads, preferred_element_type=jnp.float32)
    carried = jnp.einsum("in,hpn->ihp", c_proj.astype(jnp.float32), state_now, precision=exact_mode)
    inter = jnp.exp(cumulative).T[:, :, None] * carried
    final_log = cumulative[:, -1]
    tail_weight = jnp.exp(final_log[:, None] - cumulative) * dt_live
    mixed_b = (tail_weight.T[:, :, None] * b_proj.astype(jnp.float32)[:, None, :]).astype(
        jnp.bfloat16
    )
    fresh_state = jnp.einsum("jhp,jhn->hpn", x_heads, mixed_b, preferred_element_type=jnp.float32)
    state_now = jnp.exp(final_log)[:, None, None] * state_now + fresh_state
    outputs = intra + inter + skip_gain[None, :, None] * x_heads.astype(jnp.float32)
    raw_rows = outputs.reshape(turn_rows, inner_width)
    gated = raw_rows * jax.nn.silu(gate_z.astype(jnp.float32))
    total_squares = lax.psum(jnp.sum(gated * gated, axis=1), "tp")
    mean_square = total_squares / (inner_width * lax.axis_size("tp"))
    normed = gated * lax.rsqrt(mean_square + EPSILON)[:, None] * norm_gain[None, :]
    mixed_out = jnp.where(live_rows[:, None], normed, 0.0).astype(jnp.bfloat16)
    return (mixed_out, state_now.reshape(1, inner_width, state_dim).astype(jnp.bfloat16))


def attention_rows(queries, new_kv, cache_kv, cached_count, length):
    turn_rows = queries.shape[0]
    cache_rows = cache_kv.shape[0]
    query_heads = queries.reshape(turn_rows, queries.shape[1] // KV_DIM, KV_DIM)
    all_keys = jnp.concatenate([cache_kv[:, :KV_DIM], new_kv[:, :KV_DIM]], axis=0)
    all_values = jnp.concatenate([cache_kv[:, KV_DIM:], new_kv[:, KV_DIM:]], axis=0)
    scores = jnp.einsum(
        "tqd,kd->qtk", query_heads, all_keys, preferred_element_type=jnp.float32
    ) * KV_DIM ** (-0.5)
    key_index = jnp.arange(cache_rows + turn_rows, dtype=jnp.int32)
    row_index = jnp.arange(turn_rows, dtype=jnp.int32)
    visible = jnp.where(
        key_index[None, :] < cache_rows,
        key_index[None, :] < cached_count,
        key_index[None, :] - cache_rows <= row_index[:, None],
    )
    masked = jnp.where(visible[None], scores, -jnp.inf)
    row_max = jnp.max(masked, axis=2, keepdims=True)
    raised = jnp.where(visible[None], jnp.exp(masked - row_max), 0.0)
    probs = (raised / jnp.sum(raised, axis=2, keepdims=True)).astype(jnp.bfloat16)
    mixed = jnp.einsum(
        "qtk,kd->tqd", probs, all_values, preferred_element_type=jnp.float32
    ).reshape(turn_rows, queries.shape[1])
    live_rows = row_index < length
    return jnp.where(live_rows[:, None], mixed, 0.0).astype(jnp.bfloat16)


def on_device(
    cached_state,
    kv_pool,
    page_table,
    cached_len,
    source_session,
    turn_len,
    x_inner,
    gate_z,
    b_proj,
    c_proj,
    step_size,
    decay_rate,
    skip_gain,
    norm_gain,
    queries,
    new_kv,
):
    instances = lax.axis_size("inst")
    own_index = lax.axis_index("inst")
    store_count = cached_state.shape[0]
    state_dim = cached_state.shape[2]
    kv_width = kv_pool.shape[2]
    cache_rows = page_table.shape[1] * kv_pool.shape[1]
    assembled = jnp.take(kv_pool, page_table.reshape(-1), axis=0).reshape(
        store_count, cache_rows, kv_width
    )
    spread_state, spread_kv = (
        lax.all_to_all(cached_state, "inst", split_axis=1, concat_axis=0, tiled=True),
        lax.all_to_all(assembled, "inst", split_axis=1, concat_axis=0, tiled=True),
    )
    piece_state = spread_state.shape[1]
    piece_tokens = spread_kv.shape[1]
    outgoing_state = jnp.take(spread_state, source_session, axis=0).reshape(
        1, instances * piece_state, state_dim
    )
    outgoing_kv = jnp.take(spread_kv, source_session, axis=0).reshape(
        1, instances * piece_tokens, kv_width
    )
    start_rows, cache_kv = (
        lax.all_to_all(outgoing_state, "inst", split_axis=1, concat_axis=1, tiled=True),
        lax.all_to_all(outgoing_kv, "inst", split_axis=1, concat_axis=1, tiled=True),
    )
    stored_id = source_session[own_index]
    cached_count = cached_len[stored_id]
    length = turn_len[0]
    head_count = step_size.shape[0]
    start_state = start_rows[0].astype(jnp.float32).reshape(head_count, HEAD_DIM, state_dim)
    mixed_out, new_state = mixer_rows(
        x_inner,
        gate_z,
        b_proj,
        c_proj,
        step_size,
        decay_rate,
        skip_gain,
        norm_gain,
        start_state,
        length,
    )
    attn_out = attention_rows(queries, new_kv, cache_kv[0], cached_count, length)
    return (mixed_out, attn_out, new_state)


def solution(mesh):
    in_specs = (
        P("inst", "tp", None),
        P("inst", None, "tp"),
        P("inst", None),
        P(),
        P(),
        P("inst"),
        P("inst", "tp"),
        P("inst", "tp"),
        P("inst", "tp"),
        P("inst", "tp"),
        P("tp", "inst"),
        P("tp"),
        P("tp"),
        P("tp"),
        P("inst", "tp"),
        P("inst", "tp"),
    )
    out_specs = (P("inst", "tp"), P("inst", "tp"), P("inst", "tp", None))
    return jax.shard_map(
        on_device, mesh=mesh, in_specs=in_specs, out_specs=out_specs, check_vma=False
    )
```

profile of v0, /device:TPU:1, one launch (start us, length us, event | category | flops | bytes accessed | tf_op | source)
XLA Modules:
  0.0 166.0 jit_solution(12672370494919299962)
XLA Ops:
  0.6 0.0 copy-start
  0.7 0.8 reshape.255
  1.5 0.7 compare_and_fusion
  2.2 0.1 broadcast_in_dim.165
  2.3 0.1 broadcast_in_dim.166
  2.4 0.6 gather_fusion.1
  3.0 0.0 copy-start.12
  3.0 0.0 copy-start.6
  3.0 0.0 copy-start.3
  3.0 0.2 bitcast_select_fusion.2
  3.2 0.0 copy-start.7
  3.3 0.0 copy-start.10
  3.3 0.0 copy-start.4
  3.3 0.0 copy-start.11
  3.3 1.3 copy.59
  4.6 19.1 %all-to-all-start.2 = ((bf16[2,512,256]{2,0,1:T(2,128)(2,1)}), bf16[2,512,256]{2,0,1:T(2,128)(2,1)S(1)}, u32[]{:S(2)}, u32[]{:S(2)}) async-start(bf16[2,512,256]{2,0,1:T(2,128)(2,1)} %copy.59), calls=%async_computation.2 | async-start | bytes 1048576 | tf_op jit(solution)/shard_map/all_to_all | solution.py:122
  23.8 1.3 copy.54
  25.1 28.7 %all-to-all-done.2 = bf16[2,512,256]{2,0,1:T(2,128)(2,1)S(1)} async-done(((bf16[2,512,256]{2,0,1:T(2,128)(2,1)}), bf16[2,512,256]{2,0,1:T(2,128)(2,1)S(1)}, u32[]{:S(2)}, u32[]{:S(2)}) %all-to-all-start.2) | async-done | bytes 524320 | tf_op jit(solution)/shard_map/all_to_all | solution.py:122
  53.8 7.9 %all-to-all-start = ((bf16[2,1024,128]{2,0,1:T(2,128)(2,1)}), bf16[2,1024,128]{2,0,1:T(2,128)(2,1)S(1)}, u32[]{:S(2)}, u32[]{:S(2)}) async-start(bf16[2,1024,128]{2,0,1:T(2,128)(2,1)} %copy.54), calls=%async_computation | async-start | bytes 1048576 | tf_op jit(solution)/shard_map/all_to_all | solution.py:121
  61.6 0.6 dynamic_slice.6
  63.5 0.1 broadcast_in_dim.162
  63.6 0.1 broadcast_in_dim.163
  63.8 0.1 copy.72
  64.5 0.1 broadcast_in_dim.156
  64.6 0.1 broadcast_in_dim.157
  64.7 0.2 copy.53
  64.9 0.2 fusion.38
  65.1 0.2 slice_reduce_fusion
  66.0 0.6 dynamic_slice.7
  66.7 0.0 copy-start.5
  66.7 0.1 copy.94
  66.8 0.6 gather_fusion.2
  67.4 3.9 %fusion.55 = bf16[512,1,256]{2,1,0:T(2,128)(2,1)S(1)} fusion(bf16[1,512,256]{2,1,0:T(8,128)(2,1)S(1)} %bitcast.109, pred[512]{0:T(512)(128)(4,1)S(1)} %broadcast_in_dim.163), kind=kLoop, calls=%fused_computation.88 | loop fusion | flops 131072 | bytes 524800
  71.3 0.5 broadcast.179
  71.9 2.3 %reduce.3 = bf16[512,256]{1,0:T(8,128)(2,1)S(1)} reduce(bf16[512,1,256]{2,1,0:T(2,128)(2,1)S(1)} %fusion.55, bf16[]{:T(256)} %broadcast.179), dimensions={1}, to_apply=%fusion.55.reduce_sub_computation | reduce | bytes 524290
  74.1 0.8 reshape.290
  74.9 16.0 %all-to-all-done = bf16[2,1024,128]{2,0,1:T(2,128)(2,1)S(1)} async-done(((bf16[2,1024,128]{2,0,1:T(2,128)(2,1)}), bf16[2,1024,128]{2,0,1:T(2,128)(2,1)S(1)}, u32[]{:S(2)}, u32[]{:S(2)}) %all-to-all-start) | async-done | bytes 524320 | tf_op jit(solution)/shard_map/all_to_all | solution.py:121
  90.9 8.8 %all-to-all-start.3 = ((bf16[64,2,1024]{2,1,0:T(2,128)(2,1)}), bf16[64,2,1024]{2,1,0:T(2,128)(2,1)S(1)}, u32[]{:S(2)}, u32[]{:S(2)}) async-start(bf16[64,2,1024]{2,1,0:T(2,128)(2,1)} %reshape.290), calls=%async_computation.3 | async-start | bytes 524288 | tf_op jit(solution)/shard_map/all_to_all | solution.py:134
  99.7 0.7 iota_compare_fusion.3
  100.4 0.1 multiply_bitcast_fusion
  100.5 0.3 fusion.23
  100.8 0.1 fusion.57
  100.9 0.1 copy.55
  101.1 0.6 gather_fusion
  101.7 7.5 %fusion.56 = bf16[1024,1,128]{2,1,0:T(2,128)(2,1)S(1)} fusion(bf16[1,1024,128]{2,1,0:T(8,128)(2,1)S(1)} %bitcast.108, pred[1024]{0:T(1024)(128)(4,1)S(1)} %broadcast_in_dim.157), kind=kLoop, calls=%fused_computation.89 | loop fusion | flops 131072 | bytes 525312
  109.3 2.2 %reduce.2 = bf16[1024,128]{1,0:T(8,128)(2,1)S(1)} reduce(bf16[1024,1,128]{2,1,0:T(2,128)(2,1)S(1)} %fusion.56, bf16[]{:T(256)} %broadcast.179), dimensions={1}, to_apply=%fusion.56.reduce_sub_computation | reduce | bytes 524290
  111.5 0.8 reshape.288
  112.2 5.7 %all-to-all-done.3 = bf16[64,2,1024]{2,1,0:T(2,128)(2,1)S(1)} async-done(((bf16[64,2,1024]{2,1,0:T(2,128)(2,1)}), bf16[64,2,1024]{2,1,0:T(2,128)(2,1)S(1)}, u32[]{:S(2)}, u32[]{:S(2)}) %all-to-all-start.3) | async-done | bytes 262176 | tf_op jit(solution)/shard_map/all_to_all | solution.py:134
  117.9 8.7 %all-to-all-start.1 = ((bf16[64,2,1024]{2,1,0:T(2,128)(2,1)}), bf16[64,2,1024]{2,1,0:T(2,128)(2,1)S(1)}, u32[]{:S(2)}, u32[]{:S(2)}) async-start(bf16[64,2,1024]{2,1,0:T(2,128)(2,1)} %reshape.288), calls=%async_computation.1 | async-start | bytes 524288 | tf_op jit(solution)/shard_map/all_to_all | solution.py:133
  126.6 0.2 reshape.291
  126.9 0.1 copy.71
  127.1 2.6 %fusion.52 = (f32[8,128]{1,0:T(8,128)S(1)}, f32[8,128,640]{1,2,0:T(8,128)}) fusion(pred[128,640]{0,1:T(8,128)(4,1)S(1)} %fusion.23, bf16[128,128]{1,0:T(8,128)(2,1)S(1)} %get-tuple-element.6, bf16[512,128]{1,0:T(8,128)(2,1)S(1)} %get-tuple-element.4, bf16[128,1024]{1,0:T(8,128)(2,1)S(1)} %copy-done.9), kind=kOutput, calls=%fused_computation.87 | convolution fusion | flops 171377280 | bytes 3133440 | tf_op jit(solution)/shard_map/sub | solution.py:84
  129.7 2.1 %fusion.4 = bf16[128,8,128]{2,0,1:T(8,128)(2,1)S(1)} fusion(f32[8,128,640]{1,2,0:T(8,128)} %get-tuple-element.10, f32[8,128]{1,0:T(8,128)S(1)} %get-tuple-element.9, bf16[128,128]{0,1:T(8,128)(2,1)S(1)} %copy.72, bf16[512,128]{0,1:T(8,128)(2,1)S(1)} %copy.71), kind=kOutput, calls=%fused_computation.10 | convolution fusion | flops 169410560 | bytes 3051520 | tf_op jit(solution)/shard_map/qtk,kd->tqd/dot_general | solution.py:86
  131.8 0.1 copy.67
  132.0 0.8 select_convert_fusion
  132.8 11.8 %all-to-all-done.1 = bf16[64,2,1024]{2,1,0:T(2,128)(2,1)S(1)} async-done(((bf16[64,2,1024]{2,1,0:T(2,128)(2,1)}), bf16[64,2,1024]{2,1,0:T(2,128)(2,1)S(1)}, u32[]{:S(2)}, u32[]{:S(2)}) %all-to-all-start.1) | async-done | bytes 262176 | tf_op jit(solution)/shard_map/all_to_all | solution.py:133
  144.6 0.2 reshape.289
  144.9 0.2 fusion.6
  145.1 0.6 fusion.8
  145.7 0.2 copy.58
  145.9 0.2 multiply_reduce_fusion
  146.2 17.6 %psum.7 = f32[128]{0:T(128)S(1)} all-reduce(f32[128]{0:T(128)S(1)} %multiply_reduce_fusion), channel_id=1, replica_groups=mesh['inst'=64,'tp'=8] {'tp'}, use_global_device_ids=true, to_apply=%region_1.2 | all-reduce | flops 128 | bytes 1024 | tf_op jit(solution)/shard_map/psum | solution.py:59
  163.8 1.0 select_convert_fusion.1
  164.8 1.2 fusion.10
  (37 shorter events, 0.3 us)
Async XLA Ops:
  0.6 1.8 %copy-start = (bf16[64,16,256]{2,1,0:T(8,128)(2,1)S(1)}, bf16[64,16,256]{2,1,0:T(8,128)(2,1)}, u32[]{:S(2)}) copy-start(bf16[64,16,256]{2,1,0:T(8,128)(2,1)} %param.17) | copy-start | bytes 1572868
  0.6 23.1 %copy-start.2 = (bf16[2,1024,128]{2,1,0:T(8,128)(2,1)S(1)}, bf16[2,1024,128]{2,1,0:T(8,128)(2,1)}, u32[]{:S(2)}) copy-start(bf16[2,1024,128]{2,1,0:T(8,128)(2,1)} %param.16) | copy-start | bytes 1572868
  3.0 58.7 %copy-start.12 = (s32[64]{0:T(128)S(1)}, s32[64]{0:T(128)}, u32[]{:S(2)}) copy-start(s32[64]{0:T(128)} %param.20) | copy-start | bytes 772
  3.0 60.7 %copy-start.6 = (bf16[128,256]{1,0:T(8,128)(2,1)S(1)}, bf16[128,256]{1,0:T(8,128)(2,1)}, u32[]{:S(2)}) copy-start(bf16[128,256]{1,0:T(8,128)(2,1)} %param.31) | copy-start | bytes 196612
  3.0 61.7 %copy-start.3 = (bf16[128,1024]{1,0:T(8,128)(2,1)S(1)}, bf16[128,1024]{1,0:T(8,128)(2,1)}, u32[]{:S(2)}) copy-start(bf16[128,1024]{1,0:T(8,128)(2,1)} %param.22) | copy-start | bytes 786436
  3.2 61.7 %copy-start.7 = (f32[16,128]{1,0:T(8,128)S(1)}, f32[16,128]{1,0:T(8,128)}, u32[]{:S(2)}) copy-start(f32[16,128]{1,0:T(8,128)} %param.26) | copy-start | bytes 24580
  3.3 61.7 %copy-start.10 = (f32[16]{0:T(128)S(1)}, f32[16]{0:T(128)}, u32[]{:S(2)}) copy-start(f32[16]{0:T(128)} %param.27) | copy-start | bytes 196
  3.3 62.1 %copy-start.4 = (bf16[128,128]{1,0:T(8,128)(2,1)S(1)}, bf16[128,128]{1,0:T(8,128)(2,1)}, u32[]{:S(2)}) copy-start(bf16[128,128]{1,0:T(8,128)(2,1)} %param.24) | copy-start | bytes 98308
  3.3 62.7 %copy-start.11 = (s32[128]{0:T(128)S(1)}, s32[128]{0:T(128)}, u32[]{:S(2)}) copy-start(s32[128]{0:T(128)} %param.19) | copy-start | bytes 1540
  4.6 49.1 %all-to-all-start.2 = ((bf16[2,512,256]{2,0,1:T(2,128)(2,1)}), bf16[2,512,256]{2,0,1:T(2,128)(2,1)S(1)}, u32[]{:S(2)}, u32[]{:S(2)}) async-start(bf16[2,512,256]{2,0,1:T(2,128)(2,1)} %copy.59), calls=%async_computation.2 | async-start | bytes 1048576 | tf_op jit(solution)/shard_map/all_to_all | solution.py:122
  53.8 37.1 %all-to-all-start = ((bf16[2,1024,128]{2,0,1:T(2,128)(2,1)}), bf16[2,1024,128]{2,0,1:T(2,128)(2,1)S(1)}, u32[]{:S(2)}, u32[]{:S(2)}) async-start(bf16[2,1024,128]{2,0,1:T(2,128)(2,1)} %copy.54), calls=%async_computation | async-start | bytes 1048576 | tf_op jit(solution)/shard_map/all_to_all | solution.py:121
  66.7 34.1 %copy-start.5 = (bf16[128,128]{1,0:T(8,128)(2,1)S(1)}, bf16[128,128]{1,0:T(8,128)(2,1)}, u32[]{:S(2)}) copy-start(bf16[128,128]{1,0:T(8,128)(2,1)} %param.25) | copy-start | bytes 98308
  90.9 27.0 %all-to-all-start.3 = ((bf16[64,2,1024]{2,1,0:T(2,128)(2,1)}), bf16[64,2,1024]{2,1,0:T(2,128)(2,1)S(1)}, u32[]{:S(2)}, u32[]{:S(2)}) async-start(bf16[64,2,1024]{2,1,0:T(2,128)(2,1)} %reshape.290), calls=%async_computation.3 | async-start | bytes 524288 | tf_op jit(solution)/shard_map/all_to_all | solution.py:134
  101.7 25.4 %copy-start.9 = (bf16[128,1024]{1,0:T(8,128)(2,1)S(1)}, bf16[128,1024]{1,0:T(8,128)(2,1)}, u32[]{:S(2)}) copy-start(bf16[128,1024]{1,0:T(8,128)(2,1)} %param.30) | copy-start | bytes 786436
  117.9 26.7 %all-to-all-start.1 = ((bf16[64,2,1024]{2,1,0:T(2,128)(2,1)}), bf16[64,2,1024]{2,1,0:T(2,128)(2,1)S(1)}, u32[]{:S(2)}, u32[]{:S(2)}) async-start(bf16[64,2,1024]{2,1,0:T(2,128)(2,1)} %reshape.288), calls=%async_computation.1 | async-start | bytes 524288 | tf_op jit(solution)/shard_map/all_to_all | solution.py:133
  131.8 13.3 %copy-start.13 = (f32[16]{0:T(128)S(1)}, f32[16]{0:T(128)}, u32[]{:S(2)}) copy-start(f32[16]{0:T(128)} %param.28) | copy-start | bytes 196
  144.8 1.1 copy-start.1
  144.9 18.9 %copy-start.8 = (f32[1024]{0:T(1024)S(1)}, f32[1024]{0:T(1024)}, u32[]{:S(2)}) copy-start(f32[1024]{0:T(1024)} %param.29) | copy-start | bytes 12292
where the time goes:
time: 167 us; the launch traced here: 166 us
  waiting for transfers between devices  62.1 us (37%)
  starting transfers between devices  44.5 us (27%)
  other arithmetic  20 us (12%)
  blocking collectives  17.6 us (11%)
  local copies, waits for them, and re-layouts  11 us (7%)
  matrix products  7.06 us (4%)
  between operations  3.75 us (2%)
    all_to_all x1, waiting for transfers between devices, on_device(): lax.all_to_all(assembled, 'inst', split_axis=1, concat_axis=0, tiled=True)  28.7 us
    all_to_all x1, starting transfers between devices, on_device(): lax.all_to_all(assembled, 'inst', split_axis=1, concat_axis=0, tiled=True)  19.1 us
    psum x1, blocking collectives, mixer_rows(): total_squares = lax.psum(jnp.sum(gated * gated, axis=1), 'tp')  17.6 us
    all_to_all x1, waiting for transfers between devices, on_device(): lax.all_to_all(cached_state, 'inst', split_axis=1, concat_axis=0, tiled=T...  16 us
    unnamed x4, other arithmetic  16 us
    all_to_all x1, waiting for transfers between devices, on_device(): lax.all_to_all(outgoing_state, 'inst', split_axis=1, concat_axis=1, tiled...  11.8 us
    all_to_all x1, starting transfers between devices, on_device(): lax.all_to_all(outgoing_kv, 'inst', split_axis=1, concat_axis=1, tiled=True)  8.8 us
    all_to_all x1, starting transfers between devices, on_device(): lax.all_to_all(outgoing_state, 'inst', split_axis=1, concat_axis=1, tiled...  8.68 us
  transfers between devices with their start and end apart: 4, of which 4 were waited for; matrix products, arithmetic and copies ran while one was open for 18% of the time, Pallas kernels for 0%

commit v1 on v0

v1 whole, which is shorter than its diff:
```python
import functools

import jax
import jax.numpy as jnp
from jax import lax
from jax.experimental import pallas as pl
from jax.experimental.pallas import tpu as pltpu
from jax.sharding import PartitionSpec as P

MESH = pl.DeviceIdType.MESH
HEAD_DIM = 64
LANES = 128
PAGE = 16
EPSILON = 1e-05
SCORE_SCALE = 128 ** (-0.5)
FAR_BELOW = -1e30


def serve_kernel(
    instances,
    ranks,
    source_ref,
    cached_len_ref,
    page_ref,
    turn_len_ref,
    rate_ref,
    skip_ref,
    state_ref,
    kv_ref,
    x_ref,
    z_ref,
    b_ref,
    c_ref,
    dt_ref,
    gain_ref,
    q_ref,
    new_ref,
    mixer_ref,
    attn_ref,
    new_state_ref,
    state_out,
    state_mid,
    state_fwd,
    state_in,
    kv_out,
    kv_mid,
    kv_fwd,
    kv_in,
    square_out,
    square_in,
    raw,
    reach,
    silu,
    fresh,
    send_sem,
    recv_sem,
    square_send,
    square_recv,
):
    me = lax.axis_index("inst")
    rank = lax.axis_index("tp")
    others = instances - 1
    barrier = pltpu.get_barrier_semaphore()

    def greet(k, carry):
        peer = lax.rem(me + k, instances)
        pl.semaphore_signal(barrier, inc=1, device_id={"inst": peer}, device_id_type=MESH)
        return carry

    lax.fori_loop(1, instances, greet, 0)

    def greet_rank(k, carry):
        peer = lax.rem(rank + k, ranks)
        pl.semaphore_signal(barrier, inc=1, device_id={"tp": peer}, device_id_type=MESH)
        return carry

    lax.fori_loop(1, ranks, greet_rank, 0)

    def find(d, found):
        g = source_ref[d]
        return found + jnp.where(lax.shift_right_logical(g, 1) == me, g & 1, 0)

    slot = lax.fori_loop(0, instances, find, jnp.int32(0))
    state_out[...] = state_ref[slot]
    for page in range(instances // 2):
        rows = kv_ref[page_ref[slot, page]]
        kv_out[2 * page] = rows[:, :LANES]
        kv_out[2 * page + 1] = rows[:, LANES:]

    pl.semaphore_wait(barrier, others + ranks - 1)

    def partner(k):
        step = (k + 2) // 2
        return lax.rem(me + instances + step * (1 - 2 * (k % 2)), instances)

    def spread(out, mid, phase):
        def send(k, carry):
            peer = partner(k)
            pltpu.make_async_remote_copy(
                src_ref=out.at[peer],
                dst_ref=mid.at[me],
                send_sem=send_sem.at[phase],
                recv_sem=recv_sem.at[phase],
                device_id={"inst": peer},
                device_id_type=MESH,
            ).start()
            return carry

        lax.fori_loop(0, others, send, 0)
        mid[me] = out[me]

    def collect(mid, fwd, arrive, phase):
        def send(k, carry):
            peer = partner(k)
            holder = lax.shift_right_logical(source_ref[peer], 1)
            fwd[peer] = mid[holder]
            pltpu.make_async_remote_copy(
                src_ref=fwd.at[peer],
                dst_ref=arrive.at[me],
                send_sem=send_sem.at[phase],
                recv_sem=recv_sem.at[phase],
                device_id={"inst": peer},
                device_id_type=MESH,
            ).start()
            return carry

        lax.fori_loop(0, others, send, 0)
        arrive[me] = mid[lax.shift_right_logical(source_ref[me], 1)]

    def arrived(buffer, phase):
        part = buffer.at[pl.ds(0, others)]
        pltpu.make_async_copy(part, part, recv_sem.at[phase]).wait()

    def sent(buffer, phase):
        part = buffer.at[pl.ds(0, others)]
        pltpu.make_async_copy(part, part, send_sem.at[phase]).wait()

    spread(state_out, state_mid, 0)
    spread(kv_out, kv_mid, 1)

    length = turn_len_ref[0]
    tokens = x_ref.shape[0]
    heads = dt_ref.shape[0]
    tiles = x_ref.shape[1] // LANES
    row_id = lax.broadcasted_iota(jnp.int32, (tokens, tokens), 0)
    col_id = lax.broadcasted_iota(jnp.int32, (tokens, tokens), 1)
    lower = row_id >= col_id
    first_head = col_id < HEAD_DIM
    head_id = lax.broadcasted_iota(jnp.int32, (heads, tokens), 0)
    token_id = lax.broadcasted_iota(jnp.int32, (heads, tokens), 1)
    rate = jnp.zeros((heads, tokens), jnp.float32)
    for h in range(heads):
        rate = jnp.where(head_id == h, rate_ref[h], rate)
    dt = jnp.where(token_id < length, dt_ref[...], 0.0)
    log_decay = -dt * rate
    cumulative = lax.dot_general(
        log_decay,
        lower.astype(jnp.float32),
        (((1,), (1,)), ((), ())),
        precision=lax.Precision.HIGHEST,
        preferred_element_type=jnp.float32,
    )
    last = jnp.broadcast_to(cumulative[:, tokens - 1 : tokens], (heads, tokens))
    tail = jnp.exp(last - cumulative) * dt
    final = jnp.exp(last)
    stacked = jnp.concatenate(
        [
            cumulative,
            jnp.exp(cumulative),
            tail,
            jnp.zeros((tokens - 3 * heads, tokens), jnp.float32),
        ],
        axis=0,
    )
    columns = jnp.transpose(stacked)

    def column(index):
        return jnp.broadcast_to(columns[:, index : index + 1], (tokens, tokens))

    b = b_ref[...]
    c = c_ref[...]
    b_wide = b.astype(jnp.float32)
    products = lax.dot_general(
        c, b, (((1,), (1,)), ((), ())), preferred_element_type=jnp.float32
    )
    for pair in range(tiles):
        span = slice(pair * LANES, (pair + 1) * LANES)
        x = x_ref[:, span]
        parts = []
        mixed = []
        for h in (2 * pair, 2 * pair + 1):
            differ = column(h) - cumulative[h : h + 1, :]
            decay = jnp.exp(jnp.where(lower, differ, FAR_BELOW))
            weights = (products * decay * dt[h : h + 1, :]).astype(jnp.bfloat16)
            parts.append(jnp.dot(weights, x, preferred_element_type=jnp.float32))
            mixed.append((column(2 * heads + h) * b_wide).astype(jnp.bfloat16))
        gain = jnp.where(first_head, skip_ref[2 * pair], skip_ref[2 * pair + 1])
        raw[:, span] = jnp.where(first_head, parts[0], parts[1]) + gain * x.astype(
            jnp.float32
        )
        reach[:, span] = jnp.where(
            first_head, column(heads + 2 * pair), column(heads + 2 * pair + 1)
        )
        z = z_ref[:, span].astype(jnp.float32)
        silu[:, span] = z / (1.0 + jnp.exp(-z))
        both = lax.dot_general(
            x,
            jnp.concatenate(mixed, axis=1),
            (((0,), (0,)), ((), ())),
            preferred_element_type=jnp.float32,
        )
        top = pair * LANES
        fresh[top : top + HEAD_DIM] = both[:HEAD_DIM, :LANES]
        fresh[top + HEAD_DIM : top + LANES] = both[HEAD_DIM:, LANES:]

    arrived(state_mid, 0)
    collect(state_mid, state_fwd, state_in, 2)
    arrived(kv_mid, 1)
    collect(kv_mid, kv_fwd, kv_in, 3)

    arrived(state_in, 2)
    state = state_in[...].reshape(x_ref.shape[1], LANES)
    total = jnp.zeros((tokens, LANES), jnp.float32)
    for pair in range(tiles):
        span = slice(pair * LANES, (pair + 1) * LANES)
        carried = lax.dot_general(
            c, state[span], (((1,), (1,)), ((), ())), preferred_element_type=jnp.float32
        )
        gated = (raw[:, span] + reach[:, span] * carried) * silu[:, span]
        raw[:, span] = gated
        total = total + gated * gated
    squares = jnp.sum(jnp.transpose(total), axis=0, keepdims=True)
    square_out[...] = jnp.broadcast_to(squares, square_out.shape)
    square_in[rank] = jnp.broadcast_to(squares, square_out.shape)

    def tell(k, carry):
        peer = lax.rem(rank + k, ranks)
        pltpu.make_async_remote_copy(
            src_ref=square_out,
            dst_ref=square_in.at[rank],
            send_sem=square_send,
            recv_sem=square_recv,
            device_id={"tp": peer},
            device_id_type=MESH,
        ).start()
        return carry

    lax.fori_loop(1, ranks, tell, 0)
    for h in range(heads):
        span = slice(h * HEAD_DIM, (h + 1) * HEAD_DIM)
        new_state_ref[span] = (
            final[h : h + 1, :] * state[span].astype(jnp.float32) + fresh[span]
        ).astype(jnp.bfloat16)

    part = square_in.at[pl.ds(0, ranks - 1)]
    pltpu.make_async_copy(part, part, square_recv).wait()
    mean = jnp.sum(square_in[...], axis=0) / (x_ref.shape[1] * ranks)
    scale = lax.rsqrt(mean + EPSILON)
    scale = jnp.transpose(jnp.broadcast_to(scale[:1], (tokens, tokens)))
    live = row_id < length
    scale = jnp.where(live, scale, 0.0)
    for pair in range(tiles):
        span = slice(pair * LANES, (pair + 1) * LANES)
        mixer_ref[:, span] = (raw[:, span] * scale * gain_ref[:, span]).astype(jnp.bfloat16)

    cached = cached_len_ref[source_ref[me]]
    keys_new = new_ref[:, :LANES]
    values_new = new_ref[:, LANES:]
    arrived(kv_in, 3)
    keys = []
    values = []
    for page in range(instances // 2):
        keys.append(kv_in[2 * page])
        values.append(kv_in[2 * page + 1])
    keys = jnp.concatenate(keys, axis=0)
    values = jnp.concatenate(values, axis=0)
    cache_rows = keys.shape[0]
    key_id = lax.broadcasted_iota(jnp.int32, (tokens, cache_rows), 1)
    seen = key_id < cached
    for head in range(tiles):
        span = slice(head * LANES, (head + 1) * LANES)
        query = q_ref[:, span]
        old = lax.dot_general(
            query, keys, (((1,), (1,)), ((), ())), preferred_element_type=jnp.float32
        )
        new = lax.dot_general(
            query, keys_new, (((1,), (1,)), ((), ())), preferred_element_type=jnp.float32
        )
        old = jnp.where(seen, old, FAR_BELOW)
        new = jnp.where(lower, new, FAR_BELOW)
        top = jnp.maximum(
            jnp.max(old, axis=1, keepdims=True), jnp.max(new, axis=1, keepdims=True)
        )
        old = jnp.exp((old - top) * SCORE_SCALE)
        new = jnp.exp((new - top) * SCORE_SCALE)
        weight = jnp.sum(old, axis=1, keepdims=True) + jnp.sum(new, axis=1, keepdims=True)
        out = jnp.dot(
            old.astype(jnp.bfloat16), values, preferred_element_type=jnp.float32
        ) + jnp.dot(new.astype(jnp.bfloat16), values_new, preferred_element_type=jnp.float32)
        attn_ref[:, span] = jnp.where(live, out / weight, 0.0).astype(jnp.bfloat16)

    sent(state_out, 0)
    sent(kv_out, 1)
    sent(state_fwd, 2)
    sent(kv_fwd, 3)
    part = square_in.at[pl.ds(0, ranks - 1)]
    pltpu.make_async_copy(part, part, square_send).wait()


def on_device(
    instances,
    ranks,
    cached_state,
    kv_pool,
    page_table,
    cached_len,
    source_session,
    turn_len,
    x_inner,
    gate_z,
    b_proj,
    c_proj,
    step_size,
    decay_rate,
    skip_gain,
    norm_gain,
    queries,
    new_kv,
):
    stores, rows, width = cached_state.shape
    piece = (instances, PAGE, LANES)
    tokens, inner = x_inner.shape
    smem = pl.BlockSpec(memory_space=pltpu.SMEM)
    vmem = pl.BlockSpec(memory_space=pltpu.VMEM)
    mixer_out, attn_out, new_state = pl.pallas_call(
        functools.partial(serve_kernel, instances, ranks),
        out_shape=(
            jax.ShapeDtypeStruct((tokens, inner), jnp.bfloat16),
            jax.ShapeDtypeStruct((tokens, inner), jnp.bfloat16),
            jax.ShapeDtypeStruct((rows, width), jnp.bfloat16),
        ),
        in_specs=[smem] * 6 + [vmem] * 10,
        out_specs=(vmem,) * 3,
        scratch_shapes=[pltpu.VMEM(piece, jnp.bfloat16)] * 8
        + [
            pltpu.VMEM((8, LANES), jnp.float32),
            pltpu.VMEM((ranks, 8, LANES), jnp.float32),
            pltpu.VMEM((tokens, inner), jnp.float32),
            pltpu.VMEM((tokens, inner), jnp.float32),
            pltpu.VMEM((tokens, inner), jnp.float32),
            pltpu.VMEM((rows, width), jnp.float32),
            pltpu.SemaphoreType.DMA((4,)),
            pltpu.SemaphoreType.DMA((4,)),
            pltpu.SemaphoreType.DMA,
            pltpu.SemaphoreType.DMA,
        ],
        compiler_params=pltpu.CompilerParams(
            collective_id=0, has_side_effects=True, vmem_limit_bytes=48 * 1024 * 1024
        ),
    )(
        source_session,
        cached_len,
        page_table,
        turn_len,
        decay_rate,
        skip_gain,
        cached_state.reshape(stores, instances, PAGE, width),
        kv_pool,
        x_inner,
        gate_z,
        b_proj,
        c_proj,
        step_size,
        norm_gain.reshape(1, inner),
        queries,
        new_kv,
    )
    return (mixer_out, attn_out, new_state.reshape(1, rows, width))


def solution(mesh):
    in_specs = (
        P("inst", "tp", None),
        P("inst", None, "tp"),
        P("inst", None),
        P(),
        P(),
        P("inst"),
        P("inst", "tp"),
        P("inst", "tp"),
        P("inst", "tp"),
        P("inst", "tp"),
        P("tp", "inst"),
        P("tp"),
        P("tp"),
        P("tp"),
        P("inst", "tp"),
        P("inst", "tp"),
    )
    out_specs = (P("inst", "tp"), P("inst", "tp"), P("inst", "tp", None))
    body = functools.partial(on_device, mesh.shape["inst"], mesh.shape["tp"])
    return jax.shard_map(
        body, mesh=mesh, in_specs=in_specs, out_specs=out_specs, check_vma=False
    )
```

time: 167 us -> 83.8 us (0.50)
  the two profiles are of different devices: /device:TPU:1 before, /device:TPU:56 now
where the time goes in v1:
time: 83.8 us; the launch traced here: 83.2 us
  Pallas kernels  69.1 us (82%)
  local copies, waits for them, and re-layouts  12.7 us (15%)
  between operations  1.35 us (2%)
    pallas_call x1, Pallas kernels, on_device(): pl.pallas_call(functools.partial(serve_kernel, instances, ranks), out_sha...  69.1 us
    unnamed x33, local copies, waits for them, and re-layouts  12.7 us

profile of v1, /device:TPU:56, one launch (start us, length us, event | category | flops | bytes accessed | tf_op | source)
XLA Modules:
  0.0 83.2 jit_solution(7093121511068827797)
XLA Ops:
  0.6 0.0 copy-start.9
  1.3 0.0 copy-start.10
  1.3 0.0 copy-start.11
  1.3 0.0 copy-done.9
  1.3 0.7 copy-done.10
  2.0 0.0 copy-done.11
  2.0 0.0 copy-start
  2.0 1.0 %copy-done = bf16[2,1024,128]{2,1,0:T(8,128)(2,1)S(1)} copy-done((bf16[2,1024,128]{2,1,0:T(8,128)(2,1)S(1)}, bf16[2,1024,128]{2,1,0:T(8,128)(2,1)}, u32[]{:S(2)}) %copy-start) | copy-done | bytes 524312
  3.0 0.0 copy-start.1
  3.0 1.0 %copy-done.1 = bf16[64,16,256]{2,1,0:T(8,128)(2,1)S(1)} copy-done((bf16[64,16,256]{2,1,0:T(8,128)(2,1)S(1)}, bf16[64,16,256]{2,1,0:T(8,128)(2,1)}, u32[]{:S(2)}) %copy-start.1) | copy-done | bytes 524312
  4.1 0.0 copy-start.2
  4.1 0.9 %copy-done.2 = bf16[128,1024]{1,0:T(8,128)(2,1)S(1)} copy-done((bf16[128,1024]{1,0:T(8,128)(2,1)S(1)}, bf16[128,1024]{1,0:T(8,128)(2,1)}, u32[]{:S(2)}) %copy-start.2) | copy-done | bytes 262168
  5.0 0.0 copy-start.3
  5.0 0.9 %copy-done.3 = bf16[128,1024]{1,0:T(8,128)(2,1)S(1)} copy-done((bf16[128,1024]{1,0:T(8,128)(2,1)S(1)}, bf16[128,1024]{1,0:T(8,128)(2,1)}, u32[]{:S(2)}) %copy-start.3) | copy-done | bytes 262168
  6.0 0.0 copy-start.4
  6.0 0.9 %copy-done.4 = bf16[128,1024]{1,0:T(8,128)(2,1)S(1)} copy-done((bf16[128,1024]{1,0:T(8,128)(2,1)S(1)}, bf16[128,1024]{1,0:T(8,128)(2,1)}, u32[]{:S(2)}) %copy-start.4) | copy-done | bytes 262168
  6.9 0.0 copy-start.5
  6.9 0.8 %copy-done.5 = bf16[128,256]{1,0:T(8,128)(2,1)S(1)} copy-done((bf16[128,256]{1,0:T(8,128)(2,1)S(1)}, bf16[128,256]{1,0:T(8,128)(2,1)}, u32[]{:S(2)}) %copy-start.5) | copy-done | bytes 65560
  7.8 0.0 copy-start.6
  7.8 0.8 copy-done.6
  8.5 0.0 copy-start.7
  8.5 0.8 copy-done.7
  9.3 0.0 copy-start.8
  9.3 0.7 copy-done.8
  10.0 0.0 copy-start.12
  10.0 0.7 copy-done.12
  10.6 0.0 copy-start.13
  10.6 0.7 copy-done.13
  11.3 0.0 copy-start.14
  11.3 0.7 copy-done.14
  11.9 69.1 %shard_map.175 = (bf16[128,1024]{1,0:T(8,128)(2,1)S(1)}, bf16[128,1024]{1,0:T(8,128)(2,1)S(1)}, bf16[1024,128]{1,0:T(8,128)(2,1)S(1)}) custom-call(s32[64]{0:T(128)S(1)} %copy-done.11, s32[128]{0:T(128)S(1)} %copy-done.12, s32[2,32]{1,0:T(2,128)S(1)} %copy-done.10, s32[1]{0:T(128)S(6)} %copy.22.turn_len_ref, f32[16]{0:T(128)S(1)} %copy-done.13, ...), custom_call_target="tpu_custom_call" | custom-call | tf_op jit(solution)/shard_map/pallas_call | solution.py:335
  81.1 0.7 copy.23
  81.8 0.7 copy.24
  82.5 0.7 copy.25
Async XLA Ops:
  0.6 0.7 copy-start.9
  1.3 0.7 copy-start.10
  1.3 0.7 copy-start.11
  2.0 1.0 %copy-start = (bf16[2,1024,128]{2,1,0:T(8,128)(2,1)S(1)}, bf16[2,1024,128]{2,1,0:T(8,128)(2,1)}, u32[]{:S(2)}) copy-start(bf16[2,1024,128]{2,1,0:T(8,128)(2,1)} %param.16) | copy-start | bytes 1572868
  3.0 1.0 %copy-start.1 = (bf16[64,16,256]{2,1,0:T(8,128)(2,1)S(1)}, bf16[64,16,256]{2,1,0:T(8,128)(2,1)}, u32[]{:S(2)}) copy-start(bf16[64,16,256]{2,1,0:T(8,128)(2,1)} %kv_ref.1) | copy-start | bytes 1572868
  4.1 0.9 %copy-start.2 = (bf16[128,1024]{1,0:T(8,128)(2,1)S(1)}, bf16[128,1024]{1,0:T(8,128)(2,1)}, u32[]{:S(2)}) copy-start(bf16[128,1024]{1,0:T(8,128)(2,1)} %x_ref.1) | copy-start | bytes 786436
  5.0 0.9 %copy-start.3 = (bf16[128,1024]{1,0:T(8,128)(2,1)S(1)}, bf16[128,1024]{1,0:T(8,128)(2,1)}, u32[]{:S(2)}) copy-start(bf16[128,1024]{1,0:T(8,128)(2,1)} %z_ref.1) | copy-start | bytes 786436
  6.0 0.9 %copy-start.4 = (bf16[128,1024]{1,0:T(8,128)(2,1)S(1)}, bf16[128,1024]{1,0:T(8,128)(2,1)}, u32[]{:S(2)}) copy-start(bf16[128,1024]{1,0:T(8,128)(2,1)} %q_ref.1) | copy-start | bytes 786436
  6.9 0.8 %copy-start.5 = (bf16[128,256]{1,0:T(8,128)(2,1)S(1)}, bf16[128,256]{1,0:T(8,128)(2,1)}, u32[]{:S(2)}) copy-start(bf16[128,256]{1,0:T(8,128)(2,1)} %new_ref.1) | copy-start | bytes 196612
  7.8 0.8 copy-start.6
  8.5 0.8 copy-start.7
  9.3 0.7 copy-start.8
  10.0 0.7 copy-start.12
  10.6 0.7 copy-start.13
  11.3 0.7 copy-start.14

commit v2 on v1

--- a/solution.py
+++ b/solution.py
@@ -14,30 +14,39 @@
 EPSILON = 1e-05
 SCORE_SCALE = 128 ** (-0.5)
 FAR_BELOW = -1e30
+N_OPERANDS = 16
+N_OUTPUTS = 3
 
 
 def serve_kernel(
     instances,
     ranks,
-    source_ref,
-    cached_len_ref,
-    page_ref,
-    turn_len_ref,
-    rate_ref,
-    skip_ref,
-    state_ref,
-    kv_ref,
-    x_ref,
-    z_ref,
-    b_ref,
-    c_ref,
-    dt_ref,
-    gain_ref,
-    q_ref,
-    new_ref,
-    mixer_ref,
-    attn_ref,
-    new_state_ref,
+    *refs,
+):
+    operands, refs = refs[:N_OPERANDS], refs[N_OPERANDS:]
+    outputs, refs = refs[:N_OUTPUTS], refs[N_OUTPUTS:]
+    held, refs = refs[:N_OPERANDS], refs[N_OPERANDS:]
+    results, refs = refs[:N_OUTPUTS], refs[N_OUTPUTS:]
+    (
+        source_ref,
+        page_ref,
+        state_ref,
+        kv_ref,
+        turn_len_ref,
+        rate_ref,
+        skip_ref,
+        x_ref,
+        b_ref,
+        c_ref,
+        dt_ref,
+        z_ref,
+        gain_ref,
+        cached_len_ref,
+        q_ref,
+        new_ref,
+    ) = held
+    mixer_ref, attn_ref, new_state_ref = results
+    (
     state_out,
     state_mid,
     state_fwd,
@@ -56,11 +65,23 @@
     recv_sem,
     square_send,
     square_recv,
-):
+    fetch_sem,
+    store_sem,
+    ) = refs
     me = lax.axis_index("inst")
     rank = lax.axis_index("tp")
     others = instances - 1
     barrier = pltpu.get_barrier_semaphore()
+    fetches = [
+        pltpu.make_async_copy(operands[i], held[i], fetch_sem.at[i])
+        for i in range(N_OPERANDS)
+    ]
+    stores = [
+        pltpu.make_async_copy(results[i], outputs[i], store_sem.at[i])
+        for i in range(N_OUTPUTS)
+    ]
+    for fetch in fetches[:4]:
+        fetch.start()
 
     def greet(k, carry):
         peer = lax.rem(me + k, instances)
@@ -76,12 +97,19 @@
 
     lax.fori_loop(1, ranks, greet_rank, 0)
 
+    for fetch in fetches[4:]:
+        fetch.start()
+    fetches[0].wait()
+
     def find(d, found):
         g = source_ref[d]
         return found + jnp.where(lax.shift_right_logical(g, 1) == me, g & 1, 0)
 
     slot = lax.fori_loop(0, instances, find, jnp.int32(0))
+    fetches[1].wait()
+    fetches[2].wait()
     state_out[...] = state_ref[slot]
+    fetches[3].wait()
     for page in range(instances // 2):
         rows = kv_ref[page_ref[slot, page]]
         kv_out[2 * page] = rows[:, :LANES]
@@ -138,6 +166,8 @@
     spread(state_out, state_mid, 0)
     spread(kv_out, kv_mid, 1)
 
+    for fetch in fetches[4:]:
+        fetch.wait()
     length = turn_len_ref[0]
     tokens = x_ref.shape[0]
     heads = dt_ref.shape[0]
@@ -252,6 +282,7 @@
             final[h : h + 1, :] * state[span].astype(jnp.float32) + fresh[span]
         ).astype(jnp.bfloat16)
 
+    stores[2].start()
     part = square_in.at[pl.ds(0, ranks - 1)]
     pltpu.make_async_copy(part, part, square_recv).wait()
     mean = jnp.sum(square_in[...], axis=0) / (x_ref.shape[1] * ranks)
@@ -262,6 +293,8 @@
     for pair in range(tiles):
         span = slice(pair * LANES, (pair + 1) * LANES)
         mixer_ref[:, span] = (raw[:, span] * scale * gain_ref[:, span]).astype(jnp.bfloat16)
+
+    stores[0].start()
 
     cached = cached_len_ref[source_ref[me]]
     keys_new = new_ref[:, :LANES]
@@ -299,12 +332,15 @@
         ) + jnp.dot(new.astype(jnp.bfloat16), values_new, preferred_element_type=jnp.float32)
         attn_ref[:, span] = jnp.where(live, out / weight, 0.0).astype(jnp.bfloat16)
 
+    stores[1].start()
     sent(state_out, 0)
     sent(kv_out, 1)
     sent(state_fwd, 2)
     sent(kv_fwd, 3)
     part = square_in.at[pl.ds(0, ranks - 1)]
     pltpu.make_async_copy(part, part, square_send).wait()
+    for store in stores:
+        store.wait()
 
 
 def on_device(
@@ -330,18 +366,38 @@
     stores, rows, width = cached_state.shape
     piece = (instances, PAGE, LANES)
     tokens, inner = x_inner.shape
-    smem = pl.BlockSpec(memory_space=pltpu.SMEM)
-    vmem = pl.BlockSpec(memory_space=pltpu.VMEM)
+    hbm = pl.BlockSpec(memory_space=pltpu.HBM)
+    operands = (
+        (source_session, pltpu.SMEM),
+        (page_table, pltpu.SMEM),
+        (cached_state.reshape(stores, instances, PAGE, width), pltpu.VMEM),
+        (kv_pool, pltpu.VMEM),
+        (turn_len, pltpu.SMEM),
+        (decay_rate, pltpu.SMEM),
+        (skip_gain, pltpu.SMEM),
+        (x_inner, pltpu.VMEM),
+        (b_proj, pltpu.VMEM),
+        (c_proj, pltpu.VMEM),
+        (step_size, pltpu.VMEM),
+        (gate_z, pltpu.VMEM),
+        (norm_gain.reshape(1, inner), pltpu.VMEM),
+        (cached_len, pltpu.SMEM),
+        (queries, pltpu.VMEM),
+        (new_kv, pltpu.VMEM),
+    )
+    results = (
+        jax.ShapeDtypeStruct((tokens, inner), jnp.bfloat16),
+        jax.ShapeDtypeStruct((tokens, inner), jnp.bfloat16),
+        jax.ShapeDtypeStruct((rows, width), jnp.bfloat16),
+    )
     mixer_out, attn_out, new_state = pl.pallas_call(
         functools.partial(serve_kernel, instances, ranks),
-        out_shape=(
-            jax.ShapeDtypeStruct((tokens, inner), jnp.bfloat16),
-            jax.ShapeDtypeStruct((tokens, inner), jnp.bfloat16),
-            jax.ShapeDtypeStruct((rows, width), jnp.bfloat16),
-        ),
-        in_specs=[smem] * 6 + [vmem] * 10,
-        out_specs=(vmem,) * 3,
-        scratch_shapes=[pltpu.VMEM(piece, jnp.bfloat16)] * 8
+        out_shape=results,
+        in_specs=[hbm] * N_OPERANDS,
+        out_specs=(pl.BlockSpec(memory_space=pl.ANY),) * N_OUTPUTS,
+        scratch_shapes=[space(array.shape, array.dtype) for array, space in operands]
+        + [pltpu.VMEM(result.shape, result.dtype) for result in results]
+        + [pltpu.VMEM(piece, jnp.bfloat16)] * 8
         + [
             pltpu.VMEM((8, LANES), jnp.float32),
             pltpu.VMEM((ranks, 8, LANES), jnp.float32),
@@ -353,28 +409,13 @@
             pltpu.SemaphoreType.DMA((4,)),
             pltpu.SemaphoreType.DMA,
             pltpu.SemaphoreType.DMA,
+            pltpu.SemaphoreType.DMA((N_OPERANDS,)),
+            pltpu.SemaphoreType.DMA((N_OUTPUTS,)),
         ],
         compiler_params=pltpu.CompilerParams(
             collective_id=0, has_side_effects=True, vmem_limit_bytes=48 * 1024 * 1024
         ),
-    )(
-        source_session,
-        cached_len,
-        page_table,
-        turn_len,
-        decay_rate,
-        skip_gain,
-        cached_state.reshape(stores, instances, PAGE, width),
-        kv_pool,
-        x_inner,
-        gate_z,
-        b_proj,
-        c_proj,
-        step_size,
-        norm_gain.reshape(1, inner),
-        queries,
-        new_kv,
-    )
+    )(*((array if array.size == 1 else pltpu.with_memory_space_constraint(array, pltpu.HBM)) for array, _ in operands))
     return (mixer_out, attn_out, new_state.reshape(1, rows, width))
 
 

time: 83.8 us -> 72.2 us (0.86)
  the two profiles are of different devices: /device:TPU:56 before, /device:TPU:48 now
where the time goes in v2:
time: 72.2 us; the launch traced here: 72.1 us
  Pallas kernels  68.7 us (95%)
  local copies, waits for them, and re-layouts  2.11 us (3%)
  between operations  1.29 us (2%)
    pallas_call x1, Pallas kernels, on_device(): pl.pallas_call(functools.partial(serve_kernel, instances, ranks), out_sha...  68.7 us
    unnamed x3, local copies, waits for them, and re-layouts  2.11 us

profile of v2, /device:TPU:48, one launch (start us, length us, event | category | flops | bytes accessed | tf_op | source)
XLA Modules:
  0.0 72.1 jit_solution(267671458855982207)
XLA Ops:
  1.3 68.7 %shard_map.175 = (bf16[128,1024]{1,0:T(8,128)(2,1)S(1)}, bf16[128,1024]{1,0:T(8,128)(2,1)S(1)}, bf16[1024,128]{1,0:T(8,128)(2,1)S(1)}) custom-call(s32[64]{0:T(128)} %refs_0_.1, s32[2,32]{1,0:T(2,128)} %refs_1_.1, bf16[2,64,16,128]{3,2,1,0:T(8,128)(2,1)} %bitcast.4, bf16[64,16,256]{2,1,0:T(8,128)(2,1)} %refs_3_.1, s32[1]{0:T(128)S(6)} %copy.22.refs_4_, ...), custom_call_target="tpu_custom_call" | custom-call | tf_op jit(solution)/shard_map/pallas_call | solution.py:393
  70.0 0.7 copy.23
  70.7 0.7 copy.24
  71.4 0.7 copy.25

commit v3 on v2

--- a/solution.py
+++ b/solution.py
@@ -15,7 +15,8 @@
 SCORE_SCALE = 128 ** (-0.5)
 FAR_BELOW = -1e30
 N_OPERANDS = 16
-N_OUTPUTS = 3
+N_OUTPUTS = 2
+ROW = 4
 
 
 def serve_kernel(
@@ -26,7 +27,6 @@
     operands, refs = refs[:N_OPERANDS], refs[N_OPERANDS:]
     outputs, refs = refs[:N_OUTPUTS], refs[N_OUTPUTS:]
     held, refs = refs[:N_OPERANDS], refs[N_OPERANDS:]
-    results, refs = refs[:N_OUTPUTS], refs[N_OUTPUTS:]
     (
         source_ref,
         page_ref,
@@ -45,7 +45,8 @@
         q_ref,
         new_ref,
     ) = held
-    mixer_ref, attn_ref, new_state_ref = results
+    rows_ref, new_state_ref = outputs
+    mixer_ref, attn_ref = rows_ref.at[0], rows_ref.at[1]
     (
     state_out,
     state_mid,
@@ -66,7 +67,9 @@
     square_send,
     square_recv,
     fetch_sem,
-    store_sem,
+    best,
+    total_weight,
+    partial_out,
     ) = refs
     me = lax.axis_index("inst")
     rank = lax.axis_index("tp")
@@ -76,26 +79,30 @@
         pltpu.make_async_copy(operands[i], held[i], fetch_sem.at[i])
         for i in range(N_OPERANDS)
     ]
-    stores = [
-        pltpu.make_async_copy(results[i], outputs[i], store_sem.at[i])
-        for i in range(N_OUTPUTS)
-    ]
     for fetch in fetches[:4]:
         fetch.start()
 
+    half = instances // 2
+    side = me // half
+    lane = me % ROW
+
+    def around(k):
+        return lax.rem(me + instances + (k + 2) // 2 * (1 - 2 * (k % 2)), instances)
+
+    def hail(peer):
+        pl.semaphore_signal(barrier, inc=1, device_id=peer, device_id_type=MESH)
+
     def greet(k, carry):
-        peer = lax.rem(me + k, instances)
-        pl.semaphore_signal(barrier, inc=1, device_id={"inst": peer}, device_id_type=MESH)
+        hail({"inst": around(k)})
         return carry
 
-    lax.fori_loop(1, instances, greet, 0)
+    lax.fori_loop(0, others, greet, 0, unroll=7)
 
     def greet_rank(k, carry):
-        peer = lax.rem(rank + k, ranks)
-        pl.semaphore_signal(barrier, inc=1, device_id={"tp": peer}, device_id_type=MESH)
+        hail({"tp": lax.rem(rank + k, ranks)})
         return carry
 
-    lax.fori_loop(1, ranks, greet_rank, 0)
+    lax.fori_loop(1, ranks, greet_rank, 0, unroll=7)
 
     for fetch in fetches[4:]:
         fetch.start()
@@ -105,7 +112,7 @@
         g = source_ref[d]
         return found + jnp.where(lax.shift_right_logical(g, 1) == me, g & 1, 0)
 
-    slot = lax.fori_loop(0, instances, find, jnp.int32(0))
+    slot = lax.fori_loop(0, instances, find, jnp.int32(0), unroll=8)
     fetches[1].wait()
     fetches[2].wait()
     state_out[...] = state_ref[slot]
@@ -115,15 +122,9 @@
         kv_out[2 * page] = rows[:, :LANES]
         kv_out[2 * page + 1] = rows[:, LANES:]
 
-    pl.semaphore_wait(barrier, others + ranks - 1)
-
-    def partner(k):
-        step = (k + 2) // 2
-        return lax.rem(me + instances + step * (1 - 2 * (k % 2)), instances)
-
     def spread(out, mid, phase):
         def send(k, carry):
-            peer = partner(k)
+            peer = around(k)
             pltpu.make_async_remote_copy(
                 src_ref=out.at[peer],
                 dst_ref=mid.at[me],
@@ -134,37 +135,46 @@
             ).start()
             return carry
 
-        lax.fori_loop(0, others, send, 0)
-        mid[me] = out[me]
-
-    def collect(mid, fwd, arrive, phase):
+        lax.fori_loop(0, others, send, 0, unroll=7)
+
+    def in_turn(k):
+        return k // ROW * ROW + (lane + k) % ROW
+
+    def collect(mid, fwd, arrive, phase, recv, target):
         def send(k, carry):
-            peer = partner(k)
-            holder = lax.shift_right_logical(source_ref[peer], 1)
-            fwd[peer] = mid[holder]
-            pltpu.make_async_remote_copy(
-                src_ref=fwd.at[peer],
-                dst_ref=arrive.at[me],
-                send_sem=send_sem.at[phase],
-                recv_sem=recv_sem.at[phase],
-                device_id={"inst": peer},
-                device_id_type=MESH,
-            ).start()
+            peer = target(k)
+
+            @pl.when(peer != me)
+            def _():
+                holder = lax.shift_right_logical(source_ref[peer], 1)
+                fwd[peer] = mid[holder]
+                pltpu.make_async_remote_copy(
+                    src_ref=fwd.at[peer],
+                    dst_ref=arrive.at[me],
+                    send_sem=send_sem.at[phase],
+                    recv_sem=recv_sem.at[recv],
+                    device_id={"inst": peer},
+                    device_id_type=MESH,
+                ).start()
+
             return carry
 
-        lax.fori_loop(0, others, send, 0)
+        lax.fori_loop(0, instances, send, 0)
         arrive[me] = mid[lax.shift_right_logical(source_ref[me], 1)]
 
-    def arrived(buffer, phase):
-        part = buffer.at[pl.ds(0, others)]
-        pltpu.make_async_copy(part, part, recv_sem.at[phase]).wait()
+    def arrived(buffer, recv, count):
+        part = buffer.at[pl.ds(0, count)]
+        pltpu.make_async_copy(part, part, recv_sem.at[recv]).wait()
 
     def sent(buffer, phase):
         part = buffer.at[pl.ds(0, others)]
         pltpu.make_async_copy(part, part, send_sem.at[phase]).wait()
 
+    pl.semaphore_wait(barrier, others + ranks - 1)
     spread(state_out, state_mid, 0)
     spread(kv_out, kv_mid, 1)
+    state_mid[me] = state_out[me]
+    kv_mid[me] = kv_out[me]
 
     for fetch in fetches[4:]:
         fetch.wait()
@@ -243,12 +253,49 @@
         fresh[top : top + HEAD_DIM] = both[:HEAD_DIM, :LANES]
         fresh[top + HEAD_DIM : top + LANES] = both[HEAD_DIM:, LANES:]
 
-    arrived(state_mid, 0)
-    collect(state_mid, state_fwd, state_in, 2)
-    arrived(kv_mid, 1)
-    collect(kv_mid, kv_fwd, kv_in, 3)
-
-    arrived(state_in, 2)
+    live = row_id < length
+    scores = functools.partial(
+        lax.dot_general,
+        dimension_numbers=(((1,), (1,)), ((), ())),
+        preferred_element_type=jnp.float32,
+    )
+
+    def attend(head, keys, values, seen):
+        old = jnp.where(seen, scores(q_ref[:, head * LANES : (head + 1) * LANES], keys), FAR_BELOW)
+        top = jnp.max(old, axis=1, keepdims=True)
+        old = jnp.exp((old - top) * SCORE_SCALE)
+        weight = jnp.sum(old, axis=1, keepdims=True)
+        out = jnp.dot(old.astype(jnp.bfloat16), values, preferred_element_type=jnp.float32)
+        wide = (tokens, LANES)
+        return jnp.broadcast_to(top, wide), jnp.broadcast_to(weight, wide), out
+
+    def merge(one, two):
+        top = jnp.maximum(one[0], two[0])
+        left = jnp.exp((one[0] - top) * SCORE_SCALE)
+        right = jnp.exp((two[0] - top) * SCORE_SCALE)
+        return top, one[1] * left + two[1] * right, one[2] * left + two[2] * right
+
+    keys_new = new_ref[:, :LANES]
+    values_new = new_ref[:, LANES:]
+    for head in range(tiles):
+        span = slice(head * LANES, (head + 1) * LANES)
+        best[:, span], total_weight[:, span], partial_out[:, span] = attend(
+            head, keys_new, values_new, lower
+        )
+
+    arrived(state_mid, 0, others)
+    collect(state_mid, state_fwd, state_in, 2, 2, in_turn)
+    arrived(kv_mid, 1, others)
+
+    @pl.when(side == 0)
+    def _():
+        collect(kv_mid, kv_fwd, kv_in, 3, 3, in_turn)
+
+    @pl.when(side == 1)
+    def _():
+        collect(kv_mid, kv_fwd, kv_in, 3, 4, in_turn)
+
+    arrived(state_in, 2, others)
     state = state_in[...].reshape(x_ref.shape[1], LANES)
     total = jnp.zeros((tokens, LANES), jnp.float32)
     for pair in range(tiles):
@@ -282,65 +329,52 @@
             final[h : h + 1, :] * state[span].astype(jnp.float32) + fresh[span]
         ).astype(jnp.bfloat16)
 
-    stores[2].start()
     part = square_in.at[pl.ds(0, ranks - 1)]
     pltpu.make_async_copy(part, part, square_recv).wait()
     mean = jnp.sum(square_in[...], axis=0) / (x_ref.shape[1] * ranks)
     scale = lax.rsqrt(mean + EPSILON)
     scale = jnp.transpose(jnp.broadcast_to(scale[:1], (tokens, tokens)))
-    live = row_id < length
     scale = jnp.where(live, scale, 0.0)
     for pair in range(tiles):
         span = slice(pair * LANES, (pair + 1) * LANES)
         mixer_ref[:, span] = (raw[:, span] * scale * gain_ref[:, span]).astype(jnp.bfloat16)
 
-    stores[0].start()
 
     cached = cached_len_ref[source_ref[me]]
-    keys_new = new_ref[:, :LANES]
-    values_new = new_ref[:, LANES:]
-    arrived(kv_in, 3)
-    keys = []
-    values = []
-    for page in range(instances // 2):
-        keys.append(kv_in[2 * page])
-        values.append(kv_in[2 * page + 1])
-    keys = jnp.concatenate(keys, axis=0)
-    values = jnp.concatenate(values, axis=0)
-    cache_rows = keys.shape[0]
-    key_id = lax.broadcasted_iota(jnp.int32, (tokens, cache_rows), 1)
-    seen = key_id < cached
-    for head in range(tiles):
-        span = slice(head * LANES, (head + 1) * LANES)
-        query = q_ref[:, span]
-        old = lax.dot_general(
-            query, keys, (((1,), (1,)), ((), ())), preferred_element_type=jnp.float32
-        )
-        new = lax.dot_general(
-            query, keys_new, (((1,), (1,)), ((), ())), preferred_element_type=jnp.float32
-        )
-        old = jnp.where(seen, old, FAR_BELOW)
-        new = jnp.where(lower, new, FAR_BELOW)
-        top = jnp.maximum(
-            jnp.max(old, axis=1, keepdims=True), jnp.max(new, axis=1, keepdims=True)
-        )
-        old = jnp.exp((old - top) * SCORE_SCALE)
-        new = jnp.exp((new - top) * SCORE_SCALE)
-        weight = jnp.sum(old, axis=1, keepdims=True) + jnp.sum(new, axis=1, keepdims=True)
-        out = jnp.dot(
-            old.astype(jnp.bfloat16), values, preferred_element_type=jnp.float32
-        ) + jnp.dot(new.astype(jnp.bfloat16), values_new, preferred_element_type=jnp.float32)
-        attn_ref[:, span] = jnp.where(live, out / weight, 0.0).astype(jnp.bfloat16)
-
-    stores[1].start()
+    key_id = lax.broadcasted_iota(jnp.int32, (tokens, half // 2 * PAGE), 1)
+    for origin in range(2):
+
+        @pl.when(side == origin)
+        def _():
+            arrived(kv_in, 3 + origin, half - 1)
+
+        @pl.when(side != origin)
+        def _():
+            arrived(kv_in, 3 + origin, half)
+
+        first = origin * half
+        keys = jnp.concatenate([kv_in[first + 2 * p] for p in range(half // 2)], axis=0)
+        values = jnp.concatenate(
+            [kv_in[first + 2 * p + 1] for p in range(half // 2)], axis=0
+        )
+        seen = key_id + first // 2 * PAGE < cached
+        for head in range(tiles):
+            span = slice(head * LANES, (head + 1) * LANES)
+            top, weight, out = merge(
+                (best[:, span], total_weight[:, span], partial_out[:, span]),
+                attend(head, keys, values, seen),
+            )
+            if origin == 0:
+                best[:, span], total_weight[:, span], partial_out[:, span] = top, weight, out
+            else:
+                attn_ref[:, span] = jnp.where(live, out / weight, 0.0).astype(jnp.bfloat16)
+
     sent(state_out, 0)
     sent(kv_out, 1)
     sent(state_fwd, 2)
     sent(kv_fwd, 3)
     part = square_in.at[pl.ds(0, ranks - 1)]
     pltpu.make_async_copy(part, part, square_send).wait()
-    for store in stores:
-        store.wait()
 
 
 def on_device(
@@ -386,17 +420,15 @@
         (new_kv, pltpu.VMEM),
     )
     results = (
-        jax.ShapeDtypeStruct((tokens, inner), jnp.bfloat16),
-        jax.ShapeDtypeStruct((tokens, inner), jnp.bfloat16),
+        jax.ShapeDtypeStruct((2, tokens, inner), jnp.bfloat16),
         jax.ShapeDtypeStruct((rows, width), jnp.bfloat16),
     )
-    mixer_out, attn_out, new_state = pl.pallas_call(
+    token_rows, new_state = pl.pallas_call(
         functools.partial(serve_kernel, instances, ranks),
         out_shape=results,
         in_specs=[hbm] * N_OPERANDS,
-        out_specs=(pl.BlockSpec(memory_space=pl.ANY),) * N_OUTPUTS,
+        out_specs=(pl.BlockSpec(memory_space=pltpu.VMEM),) * N_OUTPUTS,
         scratch_shapes=[space(array.shape, array.dtype) for array, space in operands]
-        + [pltpu.VMEM(result.shape, result.dtype) for result in results]
         + [pltpu.VMEM(piece, jnp.bfloat16)] * 8
         + [
             pltpu.VMEM((8, LANES), jnp.float32),
@@ -406,16 +438,19 @@
             pltpu.VMEM((tokens, inner), jnp.float32),
             pltpu.VMEM((rows, width), jnp.float32),
             pltpu.SemaphoreType.DMA((4,)),
-            pltpu.SemaphoreType.DMA((4,)),
+            pltpu.SemaphoreType.DMA((5,)),
             pltpu.SemaphoreType.DMA,
             pltpu.SemaphoreType.DMA,
             pltpu.SemaphoreType.DMA((N_OPERANDS,)),
-            pltpu.SemaphoreType.DMA((N_OUTPUTS,)),
+            pltpu.VMEM((tokens, inner), jnp.float32),
+            pltpu.VMEM((tokens, inner), jnp.float32),
+            pltpu.VMEM((tokens, inner), jnp.float32),
         ],
         compiler_params=pltpu.CompilerParams(
             collective_id=0, has_side_effects=True, vmem_limit_bytes=48 * 1024 * 1024
         ),
     )(*((array if array.size == 1 else pltpu.with_memory_space_constraint(array, pltpu.HBM)) for array, _ in operands))
+    mixer_out, attn_out = token_rows[0], token_rows[1]
     return (mixer_out, attn_out, new_state.reshape(1, rows, width))
 
 

time: 72.2 us -> 67.3 us (0.932)
  the two profiles are of different devices: /device:TPU:48 before, /device:TPU:96 now
where the time goes in v3:
time: 67.3 us; the launch traced here: 67.2 us
  Pallas kernels  64.4 us (96%)
  local copies, waits for them, and re-layouts  1.53 us (2%)
  between operations  1.29 us (2%)
    pallas_call x1, Pallas kernels, on_device(): pl.pallas_call(functools.partial(serve_kernel, instances, ranks), out_sha...  64.4 us

profile of v3, /device:TPU:96, one launch (start us, length us, event | category | flops | bytes accessed | tf_op | source)
XLA Modules:
  0.0 67.2 jit_solution(9751330373908829513)
XLA Ops:
  1.3 64.4 %shard_map.175 = (bf16[2,128,1024]{2,1,0:T(8,128)(2,1)S(1)}, bf16[1024,128]{1,0:T(8,128)(2,1)S(1)}) custom-call(s32[64]{0:T(128)} %refs_0_.1, s32[2,32]{1,0:T(2,128)} %refs_1_.1, bf16[2,64,16,128]{3,2,1,0:T(8,128)(2,1)} %bitcast.8, bf16[64,16,256]{2,1,0:T(8,128)(2,1)} %refs_3_.1, s32[1]{0:T(128)S(6)} %copy.20.refs_4_, f32[16]{0:T(128)} %refs_5_.1, ...), custom_call_target="tpu_custom_call" | custom-call | tf_op jit(solution)/shard_map/pallas_call | solution.py:426
  65.7 0.8 %slice_bitcast_fusion = (bf16[128,1024]{1,0:T(8,128)(2,1)}, bf16[128,1024]{1,0:T(8,128)(2,1)}) fusion(bf16[2,128,1024]{2,1,0:T(8,128)(2,1)S(1)} %get-tuple-element.5), kind=kLoop, calls=%fused_computation | loop fusion | bytes 1048576 | tf_op jit(solution)/shard_map/squeeze | solution.py:453
  66.5 0.7 %copy.21 = bf16[1,1024,128]{2,1,0:T(8,128)(2,1)} copy(bf16[1,1024,128]{2,1,0:T(8,128)(2,1)S(1)} %bitcast.7) | data formatting | bytes 524288

commit v4 on v3

--- a/solution.py
+++ b/solution.py
@@ -93,7 +93,7 @@
         pl.semaphore_signal(barrier, inc=1, device_id=peer, device_id_type=MESH)
 
     def greet(k, carry):
-        hail({"inst": around(k)})
+        hail({"inst": around(others - 1 - k)})
         return carry
 
     lax.fori_loop(0, others, greet, 0, unroll=7)
@@ -122,9 +122,12 @@
         kv_out[2 * page] = rows[:, :LANES]
         kv_out[2 * page + 1] = rows[:, LANES:]
 
+    def outward(k):
+        return around(others - 1 - k)
+
     def spread(out, mid, phase):
         def send(k, carry):
-            peer = around(k)
+            peer = outward(k)
             pltpu.make_async_remote_copy(
                 src_ref=out.at[peer],
                 dst_ref=mid.at[me],

time: 67.3 us -> 66.1 us (0.982)
  the two profiles are of different devices: /device:TPU:96 before, /device:TPU:64 now
where the time goes in v4:
time: 66.1 us; the launch traced here: 66 us
  Pallas kernels  63.2 us (96%)
  local copies, waits for them, and re-layouts  1.53 us (2%)
  between operations  1.29 us (2%)
    pallas_call x1, Pallas kernels, on_device(): pl.pallas_call(functools.partial(serve_kernel, instances, ranks), out_sha...  63.2 us

profile of v4, /device:TPU:64, one launch (start us, length us, event | category | flops | bytes accessed | tf_op | source)
XLA Modules:
  0.0 66.0 jit_solution(7947525147118206461)
XLA Ops:
  1.3 63.2 %shard_map.175 = (bf16[2,128,1024]{2,1,0:T(8,128)(2,1)S(1)}, bf16[1024,128]{1,0:T(8,128)(2,1)S(1)}) custom-call(s32[64]{0:T(128)} %refs_0_.1, s32[2,32]{1,0:T(2,128)} %refs_1_.1, bf16[2,64,16,128]{3,2,1,0:T(8,128)(2,1)} %bitcast.8, bf16[64,16,256]{2,1,0:T(8,128)(2,1)} %refs_3_.1, s32[1]{0:T(128)S(6)} %copy.20.refs_4_, f32[16]{0:T(128)} %refs_5_.1, ...), custom_call_target="tpu_custom_call" | custom-call | tf_op jit(solution)/shard_map/pallas_call | solution.py:429
  64.5 0.8 %slice_bitcast_fusion = (bf16[128,1024]{1,0:T(8,128)(2,1)}, bf16[128,1024]{1,0:T(8,128)(2,1)}) fusion(bf16[2,128,1024]{2,1,0:T(8,128)(2,1)S(1)} %get-tuple-element.5), kind=kLoop, calls=%fused_computation | loop fusion | bytes 1048576 | tf_op jit(solution)/shard_map/squeeze | solution.py:456
  65.3 0.7 %copy.21 = bf16[1,1024,128]{2,1,0:T(8,128)(2,1)} copy(bf16[1,1024,128]{2,1,0:T(8,128)(2,1)S(1)} %bitcast.7) | data formatting | bytes 524288

commit v5 on v4

--- a/solution.py
+++ b/solution.py
@@ -96,16 +96,14 @@
         hail({"inst": around(others - 1 - k)})
         return carry
 
-    lax.fori_loop(0, others, greet, 0, unroll=7)
+    lax.fori_loop(0, others, greet, 0, unroll=21)
 
     def greet_rank(k, carry):
         hail({"tp": lax.rem(rank + k, ranks)})
         return carry
 
-    lax.fori_loop(1, ranks, greet_rank, 0, unroll=7)
-
-    for fetch in fetches[4:]:
-        fetch.start()
+    lax.fori_loop(1, ranks, greet_rank, 0, unroll=21)
+
     fetches[0].wait()
 
     def find(d, found):
@@ -138,7 +136,7 @@
             ).start()
             return carry
 
-        lax.fori_loop(0, others, send, 0, unroll=7)
+        lax.fori_loop(0, others, send, 0, unroll=21)
 
     def in_turn(k):
         return k // ROW * ROW + (lane + k) % ROW
@@ -176,6 +174,8 @@
     pl.semaphore_wait(barrier, others + ranks - 1)
     spread(state_out, state_mid, 0)
     spread(kv_out, kv_mid, 1)
+    for fetch in fetches[4:]:
+        fetch.start()
     state_mid[me] = state_out[me]
     kv_mid[me] = kv_out[me]
 

time: 66.1 us -> 66.2 us (level)
  no operation moved by 1% of the time
where the time goes in v5:
time: 66.2 us; the launch traced here: 66 us
  Pallas kernels  63.2 us (95%)
  local copies, waits for them, and re-layouts  1.53 us (2%)
  between operations  1.29 us (2%)
    pallas_call x1, Pallas kernels, on_device(): pl.pallas_call(functools.partial(serve_kernel, instances, ranks), out_sha...  63.2 us

profile of v5, /device:TPU:64, one launch (start us, length us, event | category | flops | bytes accessed | tf_op | source)
XLA Modules:
  0.0 66.0 jit_solution(3606648517420556517)
XLA Ops:
  1.3 63.2 %shard_map.175 = (bf16[2,128,1024]{2,1,0:T(8,128)(2,1)S(1)}, bf16[1024,128]{1,0:T(8,128)(2,1)S(1)}) custom-call(s32[64]{0:T(128)} %refs_0_.1, s32[2,32]{1,0:T(2,128)} %refs_1_.1, bf16[2,64,16,128]{3,2,1,0:T(8,128)(2,1)} %bitcast.8, bf16[64,16,256]{2,1,0:T(8,128)(2,1)} %refs_3_.1, s32[1]{0:T(128)S(6)} %copy.20.refs_4_, f32[16]{0:T(128)} %refs_5_.1, ...), custom_call_target="tpu_custom_call" | custom-call | tf_op jit(solution)/shard_map/pallas_call | solution.py:429
  64.5 0.8 %slice_bitcast_fusion = (bf16[128,1024]{1,0:T(8,128)(2,1)}, bf16[128,1024]{1,0:T(8,128)(2,1)}) fusion(bf16[2,128,1024]{2,1,0:T(8,128)(2,1)S(1)} %get-tuple-element.5), kind=kLoop, calls=%fused_computation | loop fusion | bytes 1048576 | tf_op jit(solution)/shard_map/squeeze | solution.py:456
  65.3 0.7 %copy.21 = bf16[1,1024,128]{2,1,0:T(8,128)(2,1)} copy(bf16[1,1024,128]{2,1,0:T(8,128)(2,1)S(1)} %bitcast.7) | data formatting | bytes 524288
